TPU v7x, 32 devices: a whole 2x2x4 slice. The times are simulated.
32 devices in a mesh: tile: 8 (over z, x), spec: 4 (over y, core).
Axes of the slice: x: 2, y: 2, z: 4, core: 2. Of those that a mesh axis runs over, the one named last changes fastest.
Arguments:
- adjoint: float32 [128, 8, 32, 128], P('spec', None, 'tile'), may hold values from -6 to 6
- section_first: bfloat16 [8, 8, 128, 128], P('tile'), may hold values from -1 to 2
- section_second: bfloat16 [8, 8, 128, 128], P('tile'), may hold values from -1 to 2
- jacobian: bfloat16 [8, 8, 128, 128], P('tile'), may hold values from -0.5 to 0.5
- pattern: int32 [8, 8, 2, 2], P('tile'), may hold values 0 or 1
- counts: int32 [8, 8], P('tile'), may hold values from 1 to 512, as said below
- courant: float32 [8, 32, 128], P(None, 'tile'), may hold values from -0.45 to 0.45
- seam_codes: int32 [8, 2], P('tile'), may hold values from 0 to 1, as said below
Outputs:
- adjoint_out: float32 [128, 8, 32, 128], P('spec', None, 'tile')
Inputs may be any that keep to these rules, and one draw needn't show every extreme that they name: The active cells of tile t and level l are the first counts[t, l] of its 4 x 128 cells in row-major order. `seam_codes`: column 0 of tile t is the code of the seam between tile t and tile t + 1, column 1 that of the seam between tile t - 1 and tile t (cyclically); a 1 means that the seam reverses the order of cells along it. `pattern`: 1 where a block is present.
All inputs are finite; a program needn't handle non-finite values.
Results may differ from a plain program's by a relative error of at most 0.004.
Values may be sent and summed in bfloat16 or wider, within the bound.
A program may use at most 64 MiB of HBM per device.

v0:
```python
import jax
import jax.numpy as jnp
from jax import lax
from jax.sharding import PartitionSpec as P

NSUB = 4


section_weights = (0.4, 0.3, 0.2, 0.1)
coupling = 0.5


def passed_along(value, axis, steps):
    count = lax.axis_size(axis)
    pairs = [(source, (source + steps) % count) for source in range(count)]
    return lax.ppermute(value, axis, pairs)


def padded(block, sides, width):
    for axis, dim in sides:
        count = lax.axis_size(axis)
        forward = [(i, i + 1) for i in range(count - 1)]
        forward.append((count - 1, 0))
        backward = [(target, source) for source, target in forward]
        low = lax.ppermute(
            lax.slice_in_dim(block, block.shape[dim] - width, None, axis=dim), axis, forward
        )
        high = lax.ppermute(lax.slice_in_dim(block, 0, width, axis=dim), axis, backward)
        block = jnp.concatenate([low, block, high], axis=dim)
    return block


def transposed(matrix, field_cells):
    return jnp.einsum("lsp,slc->plc", matrix, field_cells, preferred_element_type=jnp.float32)


def section_chain(rounded, first_factor, second_factor, jac_used, offset, out_width):
    start_wide = rounded.astype(jnp.float32)
    first_y = transposed(first_factor, rounded).astype(jnp.bfloat16)
    section_u = transposed(second_factor, first_y).astype(jnp.bfloat16)
    running_sum = None
    for section in range(4):
        if section < 3:
            coupled = transposed(jac_used, section_u)
            picked = lax.dynamic_slice_in_dim(coupled, offset, out_width, 0)
        else:
            picked = transposed(lax.dynamic_slice_in_dim(jac_used, offset, out_width, 2), section_u)
        if section == 0:
            running_sum = section_weights[0] * picked
        else:
            running_sum = running_sum + section_weights[section] * picked
        if section < 3:
            mixed_term = (start_wide + coupling * coupled).astype(jnp.bfloat16)
            first_y = transposed(first_factor, mixed_term).astype(jnp.bfloat16)
            section_u = transposed(second_factor, first_y).astype(jnp.bfloat16)
    return running_sum.astype(jnp.bfloat16)


def reorder(rim_cells, seam_code):
    return jnp.where(seam_code == 1, jnp.flip(rim_cells, axis=-1), rim_cells)


def shards(adjoint, section_first, section_second, jacobian, pattern, counts, courant, seam_codes):
    species_dev, levels, rows_dev, seam_len = adjoint.shape
    species_all = jacobian.shape[2]
    block_size = species_all // pattern.shape[2]
    cell_count = rows_dev * seam_len
    first_factor = section_first[0]
    second_factor = section_second[0]
    present = jnp.repeat(jnp.repeat(pattern[0], block_size, axis=1), block_size, axis=2) == 1
    jac_used = jnp.where(present, jacobian[0], jnp.zeros_like(jacobian[0]))
    own_part = adjoint.astype(jnp.bfloat16).reshape(species_dev, levels, cell_count)
    gathered = lax.all_gather(own_part, "spec", axis=0, tiled=True)
    chemistry = section_chain(
        gathered,
        first_factor,
        second_factor,
        jac_used,
        lax.axis_index("spec") * species_dev,
        species_dev,
    )
    cell_index = jnp.arange(cell_count, dtype=jnp.int32)
    active_mask = cell_index[None, :] < counts[0][:, None]
    chem_wide = chemistry.astype(jnp.float32)
    adjoint_flat = adjoint.reshape(species_dev, levels, cell_count)
    adjoint_state = adjoint_flat + jnp.where(
        active_mask[None], chem_wide, jnp.zeros_like(chem_wide)
    )
    adjoint_state = adjoint_state.reshape(species_dev, levels, rows_dev, seam_len)
    upper_code = seam_codes[0, 0]
    lower_code = seam_codes[0, 1]
    seam_row = passed_along(courant[:, -1:, :], "tile", 1)
    lower_faces = jnp.concatenate([reorder(seam_row, lower_code), courant[:, :-1, :]], axis=1)
    rising = jnp.maximum(courant, 0.0)
    falling = jnp.minimum(lower_faces, 0.0)
    for substep in range(NSUB):
        extended = padded(adjoint_state.astype(jnp.bfloat16), (("tile", 2),), 1).astype(
            adjoint_state.dtype
        )
        below_rim = reorder(extended[:, :, :1, :], lower_code)
        above_rim = reorder(extended[:, :, -1:, :], upper_code)
        above_cells = jnp.concatenate([adjoint_state[:, :, 1:, :], above_rim], axis=2)
        below_cells = jnp.concatenate([below_rim, adjoint_state[:, :, :-1, :]], axis=2)
        adjoint_state = (
            adjoint_state
            + rising * (above_cells - adjoint_state)
            + falling * (adjoint_state - below_cells)
        )
    return adjoint_state


def solution(mesh):
    in_specs = (
        P("spec", None, "tile", None),
        P("tile", None, None, None),
        P("tile", None, None, None),
        P("tile", None, None, None),
        P("tile", None, None, None),
        P("tile", None),
        P(None, "tile", None),
        P("tile", None),
    )
    out_specs = P("spec", None, "tile", None)
    return jax.shard_map(shards, mesh=mesh, in_specs=in_specs, out_specs=out_specs, check_vma=False)
```

profile of v0, /device:TPU:0, one launch (start us, length us, event | category | flops | bytes accessed | tf_op | source)
XLA Modules:
  0.0 107.0 jit_solution(3955435669642901379)
XLA Ops:
  6.6 1.2 %convert_element_type.91 = bf16[32,8,4,128]{3,2,1,0:T(4,128)(2,1)S(1)} convert(f32[32,8,4,128]{3,2,1,0:T(4,128)} %param.8) | non-fusion elementwise | flops 131072 | bytes 786432 | tf_op jit(solution)/shard_map/convert_element_type | solution.py:72
  7.9 0.1 reshape.61
  8.0 0.8 copy.31
  8.8 3.0 %collective-permute-start.2 = (f32[8,1,128]{2,1,0:T(1,128)S(1)}, f32[8,1,128]{2,1,0:T(1,128)S(1)}, u32[]{:S(2)}, u32[]{:S(2)}) collective-permute-start(f32[8,1,128]{2,1,0:T(1,128)S(1)} %slice.90), channel_id=1, source_target_pairs={{0,4},{4,8},{8,12},{12,16},{16,20},{20,24},{24,28},{28,0},{1,5},{5... | collective-permute-start | bytes 12296 | tf_op jit(solution)/shard_map/ppermute | solution.py:16
  11.8 0.1 iota_compare_fusion
  11.9 0.6 fusion.79
  12.5 1.0 reshape.60
  13.5 0.2 copy.23
  13.7 0.1 copy.21
  13.8 0.1 broadcast_in_dim.17
  13.9 0.1 eq.39
  15.1 0.7 bitcast_select_fusion
  15.9 0.5 collective-permute-done.2
  16.4 0.1 rev.30
  16.5 11.9 %all-gather.2.cloned.1.call-done = bf16[128,8,512]{2,0,1:T(8,128)(2,1)} async-done(((bf16[32,8,512]{2,0,1:T(8,128)(2,1)}), bf16[128,8,512]{2,0,1:T(8,128)(2,1)}) %all-gather.2.cloned.1.call-update) | async-done | bytes 1048592 | tf_op jit(solution)/shard_map/all_gather | solution.py:73
  28.4 2.7 %fusion.3 = bf16[128,8,512]{0,2,1:T(8,128)(2,1)} fusion(bf16[128,8,512]{2,0,1:T(8,128)(2,1)} %all-gather.2.cloned.1.call-done, bf16[1,8,128,128]{3,2,1,0:T(8,128)(2,1)S(1)} %copy-done), kind=kOutput, calls=%fused_computation.14 | convolution fusion | flops 134742016 | bytes 2359296 | tf_op jit(solution)/shard_map/lsp,slc->plc/dot_general | solution.py:34
  31.1 2.2 %fusion.14 = f32[8,512,128]{1,2,0:T(8,128)S(1)} fusion(bf16[8,128,128]{1,2,0:T(8,128)(2,1)} %bitcast_select_fusion, bf16[128,8,512]{0,2,1:T(8,128)(2,1)} %fusion.3, bf16[1,8,128,128]{3,2,1,0:T(8,128)(2,1)} %param.10), kind=kOutput, calls=%fused_computation.25 | convolution fusion | flops 268959744 | bytes 3670016 | tf_op jit(solution)/shard_map/lsp,slc->plc/dot_general | solution.py:34
  33.3 1.5 %fusion.5 = bf16[128,8,512]{0,2,1:T(8,128)(2,1)} fusion(bf16[128,8,512]{2,0,1:T(8,128)(2,1)S(1)} %copy-done.1, f32[8,512,128]{1,2,0:T(8,128)S(1)} %fusion.14, bf16[1,8,128,128]{3,2,1,0:T(8,128)(2,1)S(1)} %copy-done), kind=kOutput, calls=%fused_computation.16 | convolution fusion | flops 136839168 | bytes 4456448 | tf_op jit(solution)/shard_map/lsp,slc->plc/dot_general | solution.py:34
  34.8 3.4 %fusion.13 = f32[8,512,128]{1,2,0:T(8,128)} fusion(bf16[8,128,128]{1,2,0:T(8,128)(2,1)} %bitcast_select_fusion, bf16[128,8,512]{0,2,1:T(8,128)(2,1)} %fusion.5, bf16[1,8,128,128]{3,2,1,0:T(8,128)(2,1)} %param.10), kind=kOutput, calls=%fused_computation.24 | convolution fusion | flops 268959744 | bytes 3670016 | tf_op jit(solution)/shard_map/lsp,slc->plc/dot_general | solution.py:34
  38.3 3.2 %fusion.7 = bf16[128,8,512]{0,2,1:T(8,128)(2,1)} fusion(bf16[128,8,512]{2,0,1:T(8,128)(2,1)S(1)} %copy-done.1, f32[8,512,128]{1,2,0:T(8,128)} %fusion.13, bf16[1,8,128,128]{3,2,1,0:T(8,128)(2,1)S(1)} %copy-done), kind=kOutput, calls=%fused_computation.18 | convolution fusion | flops 136839168 | bytes 4456448 | tf_op jit(solution)/shard_map/lsp,slc->plc/dot_general | solution.py:34
  41.4 3.4 %fusion.12 = f32[8,512,128]{1,2,0:T(8,128)} fusion(bf16[8,128,128]{1,2,0:T(8,128)(2,1)} %bitcast_select_fusion, bf16[128,8,512]{0,2,1:T(8,128)(2,1)} %fusion.7, bf16[1,8,128,128]{3,2,1,0:T(8,128)(2,1)} %param.10), kind=kOutput, calls=%fused_computation.23 | convolution fusion | flops 268959744 | bytes 3670016 | tf_op jit(solution)/shard_map/lsp,slc->plc/dot_general | solution.py:34
  44.9 3.2 %fusion.9 = bf16[128,8,512]{0,2,1:T(8,128)(2,1)} fusion(bf16[128,8,512]{2,0,1:T(8,128)(2,1)S(1)} %copy-done.1, f32[8,512,128]{1,2,0:T(8,128)} %fusion.12, bf16[1,8,128,128]{3,2,1,0:T(8,128)(2,1)S(1)} %copy-done), kind=kOutput, calls=%fused_computation.20 | convolution fusion | flops 136839168 | bytes 4456448 | tf_op jit(solution)/shard_map/lsp,slc->plc/dot_general | solution.py:34
  48.0 2.7 %fusion.21 = f32[32,8,512]{2,0,1:T(8,128)S(1)} fusion(bf16[128,8,512]{0,2,1:T(8,128)(2,1)} %fusion.9, f32[32,8,512]{2,1,0:T(8,128)} %reshape.60, f32[8,512,128]{1,2,0:T(8,128)} %fusion.12, s32[]{:T(128)S(6)} %select_n.61, f32[8,512,128]{1,2,0:T(8,128)} %fusion.13, f32[8,512,128]{1,2,0:T(8,128)S(1)} %fusion.14, bf16[1,8,128,128]{3,2,1,0:T(8,128)(2,1)} %param.10, ...), kind=kOutput, calls=%fused_computation.32 | convolution fusion | flops 169738240 | bytes 4002816 | tf_op jit(solution)/shard_map/lsp,slc->plc/dot_general | solution.py:34
  50.8 0.2 reshape.59
  50.9 0.2 fusion.78
  51.1 1.5 %collective-permute-start = (bf16[32,8,1,128]{3,2,1,0:T(2,128)(2,1)S(1)}, bf16[32,8,1,128]{3,2,1,0:T(2,128)(2,1)S(1)}, u32[]{:S(2)}, u32[]{:S(2)}) collective-permute-start(bf16[32,8,1,128]{3,2,1,0:T(2,128)(2,1)S(1)} %get-tuple-element.33), channel_id=1, source_target_pairs={{0,4},{4,8},{8,12},{12,16},{16,20},{20,24},{24,28},{28,0},{1,5},{5... | collective-permute-start | bytes 196616 | tf_op jit(solution)/shard_map/ppermute | solution.py:25
  52.7 3.3 %collective-permute-start.1 = (bf16[32,8,1,128]{3,2,1,0:T(2,128)(2,1)S(1)}, bf16[32,8,1,128]{3,2,1,0:T(2,128)(2,1)S(1)}, u32[]{:S(2)}, u32[]{:S(2)}) collective-permute-start(bf16[32,8,1,128]{3,2,1,0:T(2,128)(2,1)S(1)} %get-tuple-element.34), channel_id=1, source_target_pairs={{4,0},{8,4},{12,8},{16,12},{20,16},{24,20},{28,24},{0,28},{5,1},{9... | collective-permute-start | bytes 196616 | tf_op jit(solution)/shard_map/ppermute | solution.py:28
  55.9 0.2 fusion.74
  56.2 3.5 %collective-permute-done = bf16[32,8,1,128]{3,2,1,0:T(2,128)(2,1)S(1)} collective-permute-done((bf16[32,8,1,128]{3,2,1,0:T(2,128)(2,1)S(1)}, bf16[32,8,1,128]{3,2,1,0:T(2,128)(2,1)S(1)}, u32[]{:S(2)}, u32[]{:S(2)}) %collective-permute-start) | collective-permute-done | bytes 65568 | tf_op jit(solution)/shard_map/ppermute | solution.py:25
  59.6 1.2 %collective-permute-done.1 = bf16[32,8,1,128]{3,2,1,0:T(2,128)(2,1)S(1)} collective-permute-done((bf16[32,8,1,128]{3,2,1,0:T(2,128)(2,1)S(1)}, bf16[32,8,1,128]{3,2,1,0:T(2,128)(2,1)S(1)}, u32[]{:S(2)}, u32[]{:S(2)}) %collective-permute-start.1) | collective-permute-done | bytes 65568 | tf_op jit(solution)/shard_map/ppermute | solution.py:28
  60.8 0.7 maximum_convert_fusion.3
  61.6 0.6 rev.31
  62.2 0.6 rev.29
  62.8 0.6 fusion.69
  63.4 0.2 fusion.77
  63.6 0.3 collective-permute-start.3
  64.0 4.4 %collective-permute-start.4 = (bf16[32,8,1,128]{3,2,1,0:T(2,128)(2,1)S(1)}, bf16[32,8,1,128]{3,2,1,0:T(2,128)(2,1)S(1)}, u32[]{:S(2)}, u32[]{:S(2)}) collective-permute-start(bf16[32,8,1,128]{3,2,1,0:T(2,128)(2,1)S(1)} %get-tuple-element.32), channel_id=1, source_target_pairs={{4,0},{8,4},{12,8},{16,12},{20,16},{24,20},{28,24},{0,28},{5,1},{9... | collective-permute-start | bytes 196616 | tf_op jit(solution)/shard_map/ppermute | solution.py:28
  68.4 0.3 fusion.73
  68.7 2.7 %collective-permute-done.3 = bf16[32,8,1,128]{3,2,1,0:T(2,128)(2,1)S(1)} collective-permute-done((bf16[32,8,1,128]{3,2,1,0:T(2,128)(2,1)S(1)}, bf16[32,8,1,128]{3,2,1,0:T(2,128)(2,1)S(1)}, u32[]{:S(2)}, u32[]{:S(2)}) %collective-permute-start.3) | collective-permute-done | bytes 65568 | tf_op jit(solution)/shard_map/ppermute | solution.py:25
  71.4 1.1 %collective-permute-done.4 = bf16[32,8,1,128]{3,2,1,0:T(2,128)(2,1)S(1)} collective-permute-done((bf16[32,8,1,128]{3,2,1,0:T(2,128)(2,1)S(1)}, bf16[32,8,1,128]{3,2,1,0:T(2,128)(2,1)S(1)}, u32[]{:S(2)}, u32[]{:S(2)}) %collective-permute-start.4) | collective-permute-done | bytes 65568 | tf_op jit(solution)/shard_map/ppermute | solution.py:28
  72.5 0.8 maximum_convert_fusion.2
  73.3 0.6 rev.32
  73.9 0.6 rev.33
  74.6 0.6 fusion.67
  75.2 0.2 fusion.76
  75.4 0.2 collective-permute-start.5
  75.6 4.7 %collective-permute-start.6 = (bf16[32,8,1,128]{3,2,1,0:T(2,128)(2,1)S(1)}, bf16[32,8,1,128]{3,2,1,0:T(2,128)(2,1)S(1)}, u32[]{:S(2)}, u32[]{:S(2)}) collective-permute-start(bf16[32,8,1,128]{3,2,1,0:T(2,128)(2,1)S(1)} %get-tuple-element.30), channel_id=1, source_target_pairs={{4,0},{8,4},{12,8},{16,12},{20,16},{24,20},{28,24},{0,28},{5,1},{9... | collective-permute-start | bytes 196616 | tf_op jit(solution)/shard_map/ppermute | solution.py:28
  80.3 0.3 fusion.72
  80.7 2.7 %collective-permute-done.5 = bf16[32,8,1,128]{3,2,1,0:T(2,128)(2,1)S(1)} collective-permute-done((bf16[32,8,1,128]{3,2,1,0:T(2,128)(2,1)S(1)}, bf16[32,8,1,128]{3,2,1,0:T(2,128)(2,1)S(1)}, u32[]{:S(2)}, u32[]{:S(2)}) %collective-permute-start.5) | collective-permute-done | bytes 65568 | tf_op jit(solution)/shard_map/ppermute | solution.py:25
  83.3 1.4 %collective-permute-done.6 = bf16[32,8,1,128]{3,2,1,0:T(2,128)(2,1)S(1)} collective-permute-done((bf16[32,8,1,128]{3,2,1,0:T(2,128)(2,1)S(1)}, bf16[32,8,1,128]{3,2,1,0:T(2,128)(2,1)S(1)}, u32[]{:S(2)}, u32[]{:S(2)}) %collective-permute-start.6) | collective-permute-done | bytes 65568 | tf_op jit(solution)/shard_map/ppermute | solution.py:28
  84.8 0.8 maximum_convert_fusion.1
  85.5 0.6 rev.34
  86.1 0.6 rev.35
  86.8 0.6 fusion.65
  87.4 0.2 fusion.75
  87.6 0.1 collective-permute-start.7
  87.6 4.7 %collective-permute-start.8 = (bf16[32,8,1,128]{3,2,1,0:T(2,128)(2,1)S(1)}, bf16[32,8,1,128]{3,2,1,0:T(2,128)(2,1)S(1)}, u32[]{:S(2)}, u32[]{:S(2)}) collective-permute-start(bf16[32,8,1,128]{3,2,1,0:T(2,128)(2,1)S(1)} %get-tuple-element.28), channel_id=1, source_target_pairs={{4,0},{8,4},{12,8},{16,12},{20,16},{24,20},{28,24},{0,28},{5,1},{9... | collective-permute-start | bytes 196616 | tf_op jit(solution)/shard_map/ppermute | solution.py:28
  92.4 0.3 fusion.71
  92.7 2.7 %collective-permute-done.7 = bf16[32,8,1,128]{3,2,1,0:T(2,128)(2,1)S(1)} collective-permute-done((bf16[32,8,1,128]{3,2,1,0:T(2,128)(2,1)S(1)}, bf16[32,8,1,128]{3,2,1,0:T(2,128)(2,1)S(1)}, u32[]{:S(2)}, u32[]{:S(2)}) %collective-permute-start.7) | collective-permute-done | bytes 65568 | tf_op jit(solution)/shard_map/ppermute | solution.py:25
  95.4 1.4 %collective-permute-done.8 = bf16[32,8,1,128]{3,2,1,0:T(2,128)(2,1)S(1)} collective-permute-done((bf16[32,8,1,128]{3,2,1,0:T(2,128)(2,1)S(1)}, bf16[32,8,1,128]{3,2,1,0:T(2,128)(2,1)S(1)}, u32[]{:S(2)}, u32[]{:S(2)}) %collective-permute-start.8) | collective-permute-done | bytes 65568 | tf_op jit(solution)/shard_map/ppermute | solution.py:28
  96.8 0.8 fusion.56
  97.6 0.6 rev.37
  98.2 0.6 rev.36
  98.8 1.3 %fusion.42 = f32[32,8,4,128]{3,2,1,0:T(4,128)} fusion(f32[32,8,4,128]{3,2,1,0:T(4,128)S(1)} %get-tuple-element.6, f32[32,8,1,128]{3,2,1,0:T(1,128)S(1)} %bitcast.131, f32[32,8,3,128]{3,2,1,0:T(4,128)S(1)} %get-tuple-element.14, f32[32,8,3,128]{3,2,1,0:T(4,128)S(1)} %get-tuple-element.13, f32[32,8,1,128]{3,2,1,0:T(1,128)S(1)} %bitcast.130, ...), kind=kLoop, calls=%fused_computation.57 | loop fusion | flops 1048576 | bytes 2129920 | tf_op jit(solution)/shard_map/add | solution.py:105
  (31 shorter events, 0.3 us)
Async XLA Ops:
  6.5 21.9 %copy-start = (bf16[1,8,128,128]{3,2,1,0:T(8,128)(2,1)S(1)}, bf16[1,8,128,128]{3,2,1,0:T(8,128)(2,1)}, u32[]{:S(2)}) copy-start(bf16[1,8,128,128]{3,2,1,0:T(8,128)(2,1)} %param.9) | copy-start | bytes 786436
  6.5 5.9 %copy-start.2 = (f32[32,8,4,128]{3,2,1,0:T(4,128)S(1)}, f32[32,8,4,128]{3,2,1,0:T(4,128)}, u32[]{:S(2)}) copy-start(f32[32,8,4,128]{3,2,1,0:T(4,128)} %param.8) | copy-start | bytes 1572868
  6.5 2.2 %copy-start.4 = (f32[8,4,128]{2,1,0:T(4,128)S(1)}, f32[8,4,128]{2,1,0:T(4,128)}, u32[]{:S(2)}) copy-start(f32[8,4,128]{2,1,0:T(4,128)} %param.14) | copy-start | bytes 49156
  6.5 5.2 %copy-start.5 = (s32[1,8,2,2]{1,3,2,0:T(2,128)S(1)}, s32[1,8,2,2]{1,3,2,0:T(2,128)}, u32[]{:S(2)}) copy-start(s32[1,8,2,2]{1,3,2,0:T(2,128)} %param.12) | copy-start | bytes 388
  6.5 5.2 %copy-start.7 = (s32[1,8]{1,0:T(1,128)S(1)}, s32[1,8]{1,0:T(1,128)}, u32[]{:S(2)}) copy-start(s32[1,8]{1,0:T(1,128)} %param.13) | copy-start | bytes 100
  6.5 5.3 %copy-start.6 = (s32[1,2]{1,0:T(1,128)S(1)}, s32[1,2]{1,0:T(1,128)}, u32[]{:S(2)}) copy-start(s32[1,2]{1,0:T(1,128)} %param.15) | copy-start | bytes 28
  6.6 6.9 %copy-start.3 = (bf16[1,8,128,128]{3,2,1,0:T(8,128)(2,1)S(1)}, bf16[1,8,128,128]{3,2,1,0:T(8,128)(2,1)}, u32[]{:S(2)}) copy-start(bf16[1,8,128,128]{3,2,1,0:T(8,128)(2,1)} %param.11) | copy-start | bytes 786436
  6.6 21.9 %all-gather.2.cloned.1.call-start = ((), (), s32[]{:S(2)}) async-start(), calls=%async_computation | async-start | bytes 1310720 | tf_op jit(solution)/shard_map/all_gather | solution.py:73
  8.8 7.6 %collective-permute-start.2 = (f32[8,1,128]{2,1,0:T(1,128)S(1)}, f32[8,1,128]{2,1,0:T(1,128)S(1)}, u32[]{:S(2)}, u32[]{:S(2)}) collective-permute-start(f32[8,1,128]{2,1,0:T(1,128)S(1)} %slice.90), channel_id=1, source_target_pairs={{0,4},{4,8},{8,12},{12,16},{16,20},{20,24},{24,28},{28,0},{1,5},{5... | collective-permute-start | bytes 12296 | tf_op jit(solution)/shard_map/ppermute | solution.py:16
  31.1 2.2 %copy-start.1 = (bf16[128,8,512]{2,0,1:T(8,128)(2,1)S(1)}, bf16[128,8,512]{2,0,1:T(8,128)(2,1)}, u32[]{:S(2)}) copy-start(bf16[128,8,512]{2,0,1:T(8,128)(2,1)} %all-gather.2.cloned.1.call-done) | copy-start | bytes 3145732
  51.1 8.5 %collective-permute-start = (bf16[32,8,1,128]{3,2,1,0:T(2,128)(2,1)S(1)}, bf16[32,8,1,128]{3,2,1,0:T(2,128)(2,1)S(1)}, u32[]{:S(2)}, u32[]{:S(2)}) collective-permute-start(bf16[32,8,1,128]{3,2,1,0:T(2,128)(2,1)S(1)} %get-tuple-element.33), channel_id=1, source_target_pairs={{0,4},{4,8},{8,12},{12,16},{16,20},{20,24},{24,28},{28,0},{1,5},{5... | collective-permute-start | bytes 196616 | tf_op jit(solution)/shard_map/ppermute | solution.py:25
  52.7 8.2 %collective-permute-start.1 = (bf16[32,8,1,128]{3,2,1,0:T(2,128)(2,1)S(1)}, bf16[32,8,1,128]{3,2,1,0:T(2,128)(2,1)S(1)}, u32[]{:S(2)}, u32[]{:S(2)}) collective-permute-start(bf16[32,8,1,128]{3,2,1,0:T(2,128)(2,1)S(1)} %get-tuple-element.34), channel_id=1, source_target_pairs={{4,0},{8,4},{12,8},{16,12},{20,16},{24,20},{28,24},{0,28},{5,1},{9... | collective-permute-start | bytes 196616 | tf_op jit(solution)/shard_map/ppermute | solution.py:28
  63.6 7.8 %collective-permute-start.3 = (bf16[32,8,1,128]{3,2,1,0:T(2,128)(2,1)S(1)}, bf16[32,8,1,128]{3,2,1,0:T(2,128)(2,1)S(1)}, u32[]{:S(2)}, u32[]{:S(2)}) collective-permute-start(bf16[32,8,1,128]{3,2,1,0:T(2,128)(2,1)S(1)} %get-tuple-element.31), channel_id=1, source_target_pairs={{0,4},{4,8},{8,12},{12,16},{16,20},{20,24},{24,28},{28,0},{1,5},{5... | collective-permute-start | bytes 196616 | tf_op jit(solution)/shard_map/ppermute | solution.py:25
  64.0 8.6 %collective-permute-start.4 = (bf16[32,8,1,128]{3,2,1,0:T(2,128)(2,1)S(1)}, bf16[32,8,1,128]{3,2,1,0:T(2,128)(2,1)S(1)}, u32[]{:S(2)}, u32[]{:S(2)}) collective-permute-start(bf16[32,8,1,128]{3,2,1,0:T(2,128)(2,1)S(1)} %get-tuple-element.32), channel_id=1, source_target_pairs={{4,0},{8,4},{12,8},{16,12},{20,16},{24,20},{28,24},{0,28},{5,1},{9... | collective-permute-start | bytes 196616 | tf_op jit(solution)/shard_map/ppermute | solution.py:28
  75.4 8.0 %collective-permute-start.5 = (bf16[32,8,1,128]{3,2,1,0:T(2,128)(2,1)S(1)}, bf16[32,8,1,128]{3,2,1,0:T(2,128)(2,1)S(1)}, u32[]{:S(2)}, u32[]{:S(2)}) collective-permute-start(bf16[32,8,1,128]{3,2,1,0:T(2,128)(2,1)S(1)} %get-tuple-element.29), channel_id=1, source_target_pairs={{0,4},{4,8},{8,12},{12,16},{16,20},{20,24},{24,28},{28,0},{1,5},{5... | collective-permute-start | bytes 196616 | tf_op jit(solution)/shard_map/ppermute | solution.py:25
  75.6 9.1 %collective-permute-start.6 = (bf16[32,8,1,128]{3,2,1,0:T(2,128)(2,1)S(1)}, bf16[32,8,1,128]{3,2,1,0:T(2,128)(2,1)S(1)}, u32[]{:S(2)}, u32[]{:S(2)}) collective-permute-start(bf16[32,8,1,128]{3,2,1,0:T(2,128)(2,1)S(1)} %get-tuple-element.30), channel_id=1, source_target_pairs={{4,0},{8,4},{12,8},{16,12},{20,16},{24,20},{28,24},{0,28},{5,1},{9... | collective-permute-start | bytes 196616 | tf_op jit(solution)/shard_map/ppermute | solution.py:28
  87.6 7.8 %collective-permute-start.7 = (bf16[32,8,1,128]{3,2,1,0:T(2,128)(2,1)S(1)}, bf16[32,8,1,128]{3,2,1,0:T(2,128)(2,1)S(1)}, u32[]{:S(2)}, u32[]{:S(2)}) collective-permute-start(bf16[32,8,1,128]{3,2,1,0:T(2,128)(2,1)S(1)} %get-tuple-element.27), channel_id=1, source_target_pairs={{0,4},{4,8},{8,12},{12,16},{16,20},{20,24},{24,28},{28,0},{1,5},{5... | collective-permute-start | bytes 196616 | tf_op jit(solution)/shard_map/ppermute | solution.py:25
  87.6 9.1 %collective-permute-start.8 = (bf16[32,8,1,128]{3,2,1,0:T(2,128)(2,1)S(1)}, bf16[32,8,1,128]{3,2,1,0:T(2,128)(2,1)S(1)}, u32[]{:S(2)}, u32[]{:S(2)}) collective-permute-start(bf16[32,8,1,128]{3,2,1,0:T(2,128)(2,1)S(1)} %get-tuple-element.28), channel_id=1, source_target_pairs={{4,0},{8,4},{12,8},{16,12},{20,16},{24,20},{28,24},{0,28},{5,1},{9... | collective-permute-start | bytes 196616 | tf_op jit(solution)/shard_map/ppermute | solution.py:28
Sparse Core Ops, SparseCore 0:
  9.0 19.4 all-gather.1
where the time goes:
time: 107 us
  waiting for transfers between devices  29.1 us (27%)
  starting transfers between devices  22.3 us (21%)
  matrix products  22.3 us (21%)
  between operations  14.9 us (14%)
  local copies, waits for them, and re-layouts  9.97 us (9%)
  other arithmetic  8.42 us (8%)
    dot_general x8, matrix products, transposed(): jnp.einsum('lsp,slc->plc', matrix, field_cells, preferred_element_type=jn...  22.3 us
    ppermute x4, starting transfers between devices, padded(): lax.ppermute(lax.slice_in_dim(block, 0, width, axis=dim), axis, backward)  17.1 us
    all_gather x1, waiting for transfers between devices, shards(): gathered = lax.all_gather(own_part, 'spec', axis=0, tiled=True)  11.9 us
    ppermute x4, waiting for transfers between devices, padded(): lax.ppermute(lax.slice_in_dim(block, block.shape[dim] - width, None, axis...  11.5 us
    ppermute x4, waiting for transfers between devices, padded(): lax.ppermute(lax.slice_in_dim(block, 0, width, axis=dim), axis, backward)  5.17 us
    rev x9, local copies, waits for them, and re-layouts, reorder(): return jnp.where(seam_code == 1, jnp.flip(rim_cells, axis=-1), rim_cells)  4.9 us
    ppermute x1, starting transfers between devices, passed_along(): return lax.ppermute(value, axis, pairs)  2.99 us
    slice x3, other arithmetic, shards(): above_rim = reorder(extended[:, :, -1:, :], upper_code)  2.31 us
  transfers between devices with their start and end apart: 10, of which 10 were waited for; matrix products, arithmetic and copies ran while one was open for 4% of the time, Pallas kernels for 0%

commit v1 on v0

v1 whole, which is shorter than its diff:
```python
import functools

import jax
import jax.numpy as jnp
from jax import lax
from jax.experimental import pallas as pl
from jax.experimental.pallas import tpu as pltpu
from jax.sharding import PartitionSpec as P

NSUB = 4

section_weights = (0.4, 0.3, 0.2, 0.1)
coupling = 0.5

MESH = pl.DeviceIdType.MESH
F32 = jnp.float32
BF16 = jnp.bfloat16


def power_weights():
    out = []
    for j in range(4):
        out.append((coupling**j) * sum(section_weights[j:]))
    return out


def dot(a, b):
    return jnp.dot(a, b, preferred_element_type=F32)


def split(x):
    hi = x.astype(BF16)
    return hi, (x - hi.astype(F32)).astype(BF16)


def kernel(
    tiles, specs, levels, rows, species_dev, blocks,
    adj_hbm, first_hbm, second_hbm, jac_hbm, cour, pattern, counts, codes,
    out,
    adj, mats, abuf, gath, ebuf, emat, sbuf, side, state, ret, rbuf,
    load_sem, a_send, a_recv, e_send, e_recv, s_send, s_recv, r_send, r_recv,
):
    seam = adj.shape[1]
    species = specs * species_dev
    cells = rows * seam
    stride = levels * rows
    pairs = tiles // 2
    t = lax.axis_index("tile")
    s = lax.axis_index("spec")
    z = t // 2
    p = t - 2 * z
    zn = lax.rem(z + pairs - 1 + 2 * p, pairs)
    slot_own = 1 + p
    slot_other = 2 - p
    slot_far = 3 * (1 - p)
    own_level = 2 * s + p

    adj_copy = pltpu.make_async_copy(adj_hbm, adj, load_sem.at[0])
    adj_copy.start()
    mat_copies = []
    for i, ref in enumerate((first_hbm, second_hbm, jac_hbm)):
        copy = pltpu.make_async_copy(ref.at[0, pl.ds(2 * s, 2)], mats.at[i], load_sem.at[1 + i])
        copy.start()
        mat_copies.append(copy)

    barrier = pltpu.get_barrier_semaphore()
    for d in range(1, levels):
        lev = lax.rem(own_level + d, levels)
        pl.semaphore_signal(barrier, inc=1, device_id=(2 * z + lax.rem(lev, 2), lev // 2), device_id_type=MESH)
    for src in range(specs):
        below = lax.rem(2 * z + tiles - 1, tiles)
        above = lax.rem(2 * z + 2, tiles)
        for q in (below, above):
            pl.semaphore_signal(barrier, inc=1, device_id=(q, src), device_id_type=MESH)

    side_rows = sbuf.shape[1]
    row_id = lax.broadcasted_iota(jnp.int32, (side_rows, seam), 0)
    for q in range(2):
        packed = jnp.where(row_id == rows, codes[0, 0].astype(F32), 0.0)
        packed = jnp.where(row_id == rows + 1, codes[0, 1].astype(F32), packed)
        packed = jnp.where(row_id == rows + 2, counts[0, 2 * s + q].astype(F32), packed)
        sbuf[q] = packed
        sbuf[q, 0:rows, :] = cour[2 * s + q]
    adj_copy.wait()
    for lev in range(levels):
        for r in range(rows):
            abuf[lev, r] = adj[pl.ds(lev * rows + r, species_dev, stride), :].astype(BF16)

    pl.semaphore_wait(barrier, 2 * levels - 1)

    sends = []

    def send(src, dst, send_sem, recv_sem, device):
        copy = pltpu.make_async_remote_copy(
            src_ref=src, dst_ref=dst, send_sem=send_sem, recv_sem=recv_sem,
            device_id=device, device_id_type=MESH,
        )
        copy.start()
        sends.append(copy)

    def owner(pair, lev):
        return (2 * pair + lax.rem(lev, 2), lev // 2)

    for d in range(levels):
        lev = lax.rem(own_level + d, levels)
        send(abuf.at[lev], gath.at[slot_far, s], a_send.at[0, d], a_recv.at[slot_far, s], owner(zn, lev))
        if d > 0:
            send(abuf.at[lev], gath.at[slot_own, s], a_send.at[1, d], a_recv.at[slot_own, s], owner(z, lev))
    targets = ((1 - p, (2 * z + 1 - p, s), slot_own), (0, (2 * zn, s), slot_far), (1, (2 * zn + 1, s), slot_far))
    for i, (q, device, slot) in enumerate(targets):
        send(sbuf.at[q], side.at[slot], s_send.at[i], s_recv.at[slot], device)

    gath[slot_own, s] = abuf[own_level]
    side[slot_own] = sbuf[p]

    for copy in mat_copies:
        copy.wait()
    weights = power_weights()
    block = species // blocks
    row_s = lax.broadcasted_iota(jnp.int32, (species, species), 0)
    col_s = lax.broadcasted_iota(jnp.int32, (species, species), 1)
    jac_used = []
    for q in range(2):
        present = jnp.zeros((species, species), jnp.int32)
        for b in range(blocks):
            for e in range(blocks):
                inside = (
                    (row_s >= b * block) & (row_s < (b + 1) * block)
                    & (col_s >= e * block) & (col_s < (e + 1) * block)
                )
                present = jnp.where(inside, pattern[0, 2 * s + q, b, e], present)
        jac_used.append(jnp.where(present == 1, mats[2, q].astype(F32), 0.0).astype(BF16))
    both = [split(dot(mats[0, q], mats[1, q])) for q in range(2)]
    g = [dot(both[q][0], jac_used[q]) + dot(both[q][1], jac_used[q]) for q in range(2)]
    gh = [g[q].astype(BF16) for q in range(2)]
    acc = [weights[2] * g[q] + weights[3] * dot(gh[q], gh[q]) for q in range(2)]
    acc = [weights[1] * g[q] + dot(gh[q], acc[q].astype(BF16)) for q in range(2)]
    acc = [weights[0] * g[q] + dot(gh[q], acc[q].astype(BF16)) for q in range(2)]
    for q in range(2):
        ebuf[q] = jnp.transpose(acc[q]).astype(BF16)
    for i, (q, device, slot) in enumerate(targets):
        send(ebuf.at[q], emat.at[slot], e_send.at[i], e_recv.at[slot], device)
    emat[slot_own] = ebuf[p]

    def arrived(dst, sem):
        pltpu.make_async_copy(dst, dst, sem).wait()

    for slot in (slot_other, 0, 3):
        arrived(side.at[slot], s_recv.at[slot])

    code_up1 = side[1, rows : rows + 1, :]
    code_down1 = side[1, rows + 1 : rows + 2, :]
    code_up2 = side[2, rows : rows + 1, :]
    flips = [code_down1, jnp.zeros_like(code_up1), code_up1, jnp.abs(code_up1 - code_up2)]
    row_y = lax.broadcasted_iota(jnp.int32, (seam, seam), 0)
    col_y = lax.broadcasted_iota(jnp.int32, (seam, seam), 1)
    eye = jnp.where(row_y == col_y, 1.0, 0.0)
    anti = jnp.where(row_y + col_y == seam - 1, 1.0, 0.0)
    perms = [(eye + (anti - eye) * flips[k]).astype(BF16) for k in range(4)]
    faces = []
    for k in range(4):
        block_k = side[k]
        if k != 1:
            hi = block_k.astype(BF16)
            rest = block_k - hi.astype(F32)
            mid = rest.astype(BF16)
            low = (rest - mid.astype(F32)).astype(BF16)
            block_k = dot(hi, perms[k]) + dot(mid, perms[k]) + dot(low, perms[k])
        for r in range(rows):
            faces.append(block_k[r : r + 1, :])

    lane = lax.broadcasted_iota(jnp.int32, (1, seam), 1).astype(F32)

    for slot in (slot_other, 0, 3):
        arrived(emat.at[slot], e_recv.at[slot])
    for d in range(1, specs):
        src = lax.rem(s + d, specs)
        arrived(gath.at[slot_own, src], a_recv.at[slot_own, src])
    for src in range(specs):
        for slot in (slot_other, 0, 3):
            arrived(gath.at[slot, src], a_recv.at[slot, src])

    for k in (1, 2, 0, 3):
        field = [[gath[k, src, r] for src in range(specs)] for r in range(rows)]
        field = [jnp.concatenate(parts, axis=0) for parts in field]
        if k != 1:
            turned = dot(jnp.concatenate(field, axis=0), perms[k]).astype(BF16)
            field = [turned[r * species : (r + 1) * species] for r in range(rows)]
        chem = dot(emat[k], jnp.concatenate(field, axis=1))
        count = side[k, rows + 2 : rows + 3, :]
        place = lane + flips[k] * (seam - 1 - 2 * lane)
        for r in range(rows):
            active = (place + float(r * seam)) < count
            term = chem[:, r * seam : (r + 1) * seam]
            state[k * rows + r] = field[r].astype(F32) + jnp.where(active, term, 0.0)

    total = 4 * rows
    group = 16
    shape = (group, seam)
    per_dev = species_dev // group

    def advect(i, carry):
        at = pl.multiple_of(i * group, group)
        a = [state[r, pl.ds(at, group), :] for r in range(total)]
        for step in range(1, NSUB + 1):
            new = list(a)
            for r in range(step, total - step):
                rising = jnp.maximum(faces[r], 0.0)
                falling = jnp.minimum(faces[r - 1], 0.0)
                new[r] = a[r] + rising * (a[r + 1] - a[r]) + falling * (a[r] - a[r - 1])
            a = new
        who = i // per_dev
        within = pl.multiple_of((i - who * per_dev) * group, group)
        for r in range(rows):
            ret[0, who, r, pl.ds(within, group), :] = a[rows + r].astype(BF16)
        upper = jnp.concatenate([a[2 * rows + r] for r in range(rows)], axis=0).astype(BF16)
        upper = dot(upper, perms[2]).astype(BF16)
        for r in range(rows):
            ret[1, who, r, pl.ds(within, group), :] = upper[r * group : (r + 1) * group]
        return carry

    lax.fori_loop(0, species // group, advect, 0)

    for d in range(1, levels):
        lev = lax.rem(own_level + d, levels)
        q = lax.rem(lev, 2)
        send(ret.at[q, lev // 2], rbuf.at[own_level], r_send.at[d], r_recv.at[own_level], owner(z, lev))
    rbuf[own_level] = ret[p, s]
    for d in range(1, levels):
        lev = lax.rem(own_level + d, levels)
        arrived(rbuf.at[lev], r_recv.at[lev])
    for lev in range(levels):
        for r in range(rows):
            out[pl.ds(lev * rows + r, species_dev, stride), :] = rbuf[lev, r].astype(F32)
    for copy in sends:
        copy.wait_send()


def shards(tiles, specs, adjoint, section_first, section_second, jacobian, pattern, counts, courant, seam_codes):
    species_dev, levels, rows, seam = adjoint.shape
    species = jacobian.shape[2]
    assert levels == 2 * specs and tiles % 2 == 0 and rows >= NSUB
    side_rows = (rows + 3 + 7) // 8 * 8
    dma = pltpu.SemaphoreType.DMA
    out = pl.pallas_call(
        functools.partial(kernel, tiles, specs, levels, rows, species_dev, pattern.shape[2]),
        out_shape=jax.ShapeDtypeStruct((species_dev * levels * rows, seam), F32),
        in_specs=[pl.BlockSpec(memory_space=pl.ANY)] * 4
        + [pl.BlockSpec(memory_space=pltpu.VMEM)]
        + [pl.BlockSpec(memory_space=pltpu.SMEM)] * 3,
        out_specs=pl.BlockSpec(memory_space=pltpu.VMEM),
        scratch_shapes=[
            pltpu.VMEM((species_dev * levels * rows, seam), F32),
            pltpu.VMEM((3, 2, species, species), BF16),
            pltpu.VMEM((levels, rows, species_dev, seam), BF16),
            pltpu.VMEM((4, specs, rows, species_dev, seam), BF16),
            pltpu.VMEM((2, species, species), BF16),
            pltpu.VMEM((4, species, species), BF16),
            pltpu.VMEM((2, side_rows, seam), F32),
            pltpu.VMEM((4, side_rows, seam), F32),
            pltpu.VMEM((4 * rows, species, seam), F32),
            pltpu.VMEM((2, specs, rows, species_dev, seam), BF16),
            pltpu.VMEM((levels, rows, species_dev, seam), BF16),
            dma((4,)),
            dma((2, levels)),
            dma((4, specs)),
            dma((3,)),
            dma((4,)),
            dma((3,)),
            dma((4,)),
            dma((levels,)),
            dma((levels,)),
        ],
        compiler_params=pltpu.CompilerParams(
            collective_id=0, has_side_effects=True, vmem_limit_bytes=32 * 1024 * 1024
        ),
    )(
        adjoint.reshape(species_dev * levels * rows, seam),
        section_first, section_second, jacobian, courant, pattern, counts, seam_codes,
    )
    return out.reshape(species_dev, levels, rows, seam)


def solution(mesh):
    in_specs = (
        P("spec", None, "tile", None),
        P("tile", None, None, None),
        P("tile", None, None, None),
        P("tile", None, None, None),
        P("tile", None, None, None),
        P("tile", None),
        P(None, "tile", None),
        P("tile", None),
    )
    out_specs = P("spec", None, "tile", None)
    body = functools.partial(shards, mesh.shape["tile"], mesh.shape["spec"])
    return jax.shard_map(body, mesh=mesh, in_specs=in_specs, out_specs=out_specs, check_vma=False)
```

time: 107 us -> 30.5 us (0.29)
  waiting for transfers between devices: 29.1 us -> 0 us
  Pallas kernels: 0 us -> 24 us
  matrix products: 22.3 us -> 0 us
  starting transfers between devices: 22.3 us -> 0 us
  between operations: 14.9 us -> 0.02 us
  other arithmetic: 8.42 us -> 0 us
  local copies, waits for them, and re-layouts: 9.97 us -> 6.2 us
    pallas_call x0 -> x1, Pallas kernels: none -> 24 us  [shards(): pl.pallas_call(functools.partial(kernel, tiles, specs, levels, rows, spec...]
    dot_general x8 -> x0, matrix products: 22.3 us -> none  [transposed(): jnp.einsum('lsp,slc->plc', matrix, field_cells, preferred_element_type=jn...]
    ppermute x9 -> x0, starting transfers between devices: 22.3 us -> none  [the longest x4 17.1 us: padded(): lax.ppermute(lax.slice_in_dim(block, 0, width, axis=dim), axis, backward)]
    ppermute x9 -> x0, waiting for transfers between devices: 17.2 us -> none  [the longest x4 11.5 us: padded(): lax.ppermute(lax.slice_in_dim(block, block.shape[dim] - width, None, axis...]
    all_gather x1 -> x0, waiting for transfers between devices: 11.9 us -> none  [shards(): gathered = lax.all_gather(own_part, 'spec', axis=0, tiled=True)]
    unnamed x17 -> x16, local copies, waits for them, and re-layouts: 0.21 us -> 6.2 us
    rev x9 -> x0, local copies, waits for them, and re-layouts: 4.9 us -> none  [reorder(): return jnp.where(seam_code == 1, jnp.flip(rim_cells, axis=-1), rim_cells)]
    convert_element_type x5 -> x0, other arithmetic: 3.8 us -> none  [the longest x3 1.79 us: shards(): adjoint_state.astype(jnp.bfloat16)]
  transfers between devices with their start and end apart: 10 -> 0, of which waited for: 10 -> 0; matrix products, arithmetic and copies ran while one was open for 4% -> 0% of each run, Pallas kernels for 0% -> 0%
where the time goes in v1:
time: 30.5 us; the launch traced here: 30.2 us
  Pallas kernels  24 us (79%)
  local copies, waits for them, and re-layouts  6.2 us (20%)
    pallas_call x1, Pallas kernels, shards(): pl.pallas_call(functools.partial(kernel, tiles, specs, levels, rows, spec...  24 us
    unnamed x16, local copies, waits for them, and re-layouts  6.2 us

profile of v1, /device:TPU:0, one launch (start us, length us, event | category | flops | bytes accessed | tf_op | source)
XLA Modules:
  0.0 30.2 jit_solution(6782340944993652129)
XLA Ops:
  0.0 0.0 copy-start.5
  0.0 0.0 copy-start.6
  0.0 0.8 %copy.9.pattern = s32[1,8,2,2]{3,2,1,0:T(2,128)S(1)} copy(s32[1,8,2,2]{1,3,2,0:T(2,128)} %param.12) | data formatting | bytes 256 | tf_op args[4]
  0.8 0.0 copy-done.5
  0.8 0.0 copy-done.6
  0.8 0.0 copy-start
  0.8 1.0 %copy-done = f32[32,8,4,128]{3,2,1,0:T(4,128)S(1)} copy-done((f32[32,8,4,128]{3,2,1,0:T(4,128)S(1)}, f32[32,8,4,128]{3,2,1,0:T(4,128)}, u32[]{:S(2)}) %copy-start) | copy-done | bytes 524312
  1.8 0.0 copy-start.1
  1.9 0.9 %copy-done.1 = bf16[1,8,128,128]{3,2,1,0:T(8,128)(2,1)S(1)} copy-done((bf16[1,8,128,128]{3,2,1,0:T(8,128)(2,1)S(1)}, bf16[1,8,128,128]{3,2,1,0:T(8,128)(2,1)}, u32[]{:S(2)}) %copy-start.1) | copy-done | bytes 262168
  2.8 0.0 copy-start.2
  2.8 0.9 %copy-done.2 = bf16[1,8,128,128]{3,2,1,0:T(8,128)(2,1)S(1)} copy-done((bf16[1,8,128,128]{3,2,1,0:T(8,128)(2,1)S(1)}, bf16[1,8,128,128]{3,2,1,0:T(8,128)(2,1)}, u32[]{:S(2)}) %copy-start.2) | copy-done | bytes 262168
  3.7 0.0 copy-start.3
  3.8 0.9 %copy-done.3 = bf16[1,8,128,128]{3,2,1,0:T(8,128)(2,1)S(1)} copy-done((bf16[1,8,128,128]{3,2,1,0:T(8,128)(2,1)S(1)}, bf16[1,8,128,128]{3,2,1,0:T(8,128)(2,1)}, u32[]{:S(2)}) %copy-start.3) | copy-done | bytes 262168
  4.7 0.0 copy-start.4
  4.7 0.7 %copy-done.4 = f32[8,4,128]{2,1,0:T(4,128)S(1)} copy-done((f32[8,4,128]{2,1,0:T(4,128)S(1)}, f32[8,4,128]{2,1,0:T(4,128)}, u32[]{:S(2)}) %copy-start.4) | copy-done | bytes 16408
  5.4 24.0 %shard_map.82 = f32[1024,128]{1,0:T(8,128)S(1)} custom-call(f32[1024,128]{1,0:T(8,128)S(1)} %bitcast.3, bf16[1,8,128,128]{3,2,1,0:T(8,128)(2,1)S(1)} %copy-done.1, bf16[1,8,128,128]{3,2,1,0:T(8,128)(2,1)S(1)} %copy-done.2, bf16[1,8,128,128]{3,2,1,0:T(8,128)(2,1)S(1)} %copy-done.3, f32[8,4,128]{2,1,0:T(4,128)S(1)} %copy-done.4, ...), custom_call_target="tpu_custom_call" | custom-call | tf_op jit(solution)/shard_map/pallas_call | solution.py:245
  29.4 0.8 %copy.11 = f32[32,8,4,128]{3,2,1,0:T(4,128)} copy(f32[32,8,4,128]{3,2,1,0:T(4,128)S(1)} %bitcast.2) | data formatting | bytes 1048576
Async XLA Ops:
  0.0 0.8 %copy-start.5 = (s32[1,8]{1,0:T(1,128)S(1)}, s32[1,8]{1,0:T(1,128)}, u32[]{:S(2)}) copy-start(s32[1,8]{1,0:T(1,128)} %counts.1) | copy-start | bytes 100
  0.0 0.8 %copy-start.6 = (s32[1,2]{1,0:T(1,128)S(1)}, s32[1,2]{1,0:T(1,128)}, u32[]{:S(2)}) copy-start(s32[1,2]{1,0:T(1,128)} %codes.1) | copy-start | bytes 28
  0.8 1.0 %copy-start = (f32[32,8,4,128]{3,2,1,0:T(4,128)S(1)}, f32[32,8,4,128]{3,2,1,0:T(4,128)}, u32[]{:S(2)}) copy-start(f32[32,8,4,128]{3,2,1,0:T(4,128)} %param.8) | copy-start | bytes 1572868
  1.8 0.9 %copy-start.1 = (bf16[1,8,128,128]{3,2,1,0:T(8,128)(2,1)S(1)}, bf16[1,8,128,128]{3,2,1,0:T(8,128)(2,1)}, u32[]{:S(2)}) copy-start(bf16[1,8,128,128]{3,2,1,0:T(8,128)(2,1)} %first_hbm.1) | copy-start | bytes 786436
  2.8 0.9 %copy-start.2 = (bf16[1,8,128,128]{3,2,1,0:T(8,128)(2,1)S(1)}, bf16[1,8,128,128]{3,2,1,0:T(8,128)(2,1)}, u32[]{:S(2)}) copy-start(bf16[1,8,128,128]{3,2,1,0:T(8,128)(2,1)} %second_hbm.1) | copy-start | bytes 786436
  3.7 0.9 %copy-start.3 = (bf16[1,8,128,128]{3,2,1,0:T(8,128)(2,1)S(1)}, bf16[1,8,128,128]{3,2,1,0:T(8,128)(2,1)}, u32[]{:S(2)}) copy-start(bf16[1,8,128,128]{3,2,1,0:T(8,128)(2,1)} %jac_hbm.1) | copy-start | bytes 786436
  4.7 0.7 %copy-start.4 = (f32[8,4,128]{2,1,0:T(4,128)S(1)}, f32[8,4,128]{2,1,0:T(4,128)}, u32[]{:S(2)}) copy-start(f32[8,4,128]{2,1,0:T(4,128)} %cour.1) | copy-start | bytes 49156

commit v2 on v1

--- a/solution.py
+++ b/solution.py
@@ -33,12 +33,16 @@
     return hi, (x - hi.astype(F32)).astype(BF16)
 
 
+def twice(x):
+    return jnp.concatenate([x, x], axis=0)
+
+
 def kernel(
     tiles, specs, levels, rows, species_dev, blocks,
-    adj_hbm, first_hbm, second_hbm, jac_hbm, cour, pattern, counts, codes,
+    adj_hbm, first_hbm, second_hbm, jac_hbm, cour_hbm, pattern_hbm, counts_hbm, codes_hbm,
     out,
-    adj, mats, abuf, gath, ebuf, emat, sbuf, side, state, ret, rbuf,
-    load_sem, a_send, a_recv, e_send, e_recv, s_send, s_recv, r_send, r_recv,
+    adj, mats, cour, pattern, counts, codes, abuf, gath, ebuf, emat, sbuf, side, state, ret,
+    load_sem, own_sem, a_send, a_recv, e_send, e_recv, s_send, s_recv, r_send, r_recv,
 ):
     seam = adj.shape[1]
     species = specs * species_dev
@@ -57,6 +61,13 @@
 
     adj_copy = pltpu.make_async_copy(adj_hbm, adj, load_sem.at[0])
     adj_copy.start()
+    small_copies = []
+    for i, (ref, to) in enumerate(
+        ((cour_hbm, cour), (counts_hbm, counts), (codes_hbm, codes), (pattern_hbm, pattern))
+    ):
+        copy = pltpu.make_async_copy(ref, to, load_sem.at[4 + i])
+        copy.start()
+        small_copies.append(copy)
     mat_copies = []
     for i, ref in enumerate((first_hbm, second_hbm, jac_hbm)):
         copy = pltpu.make_async_copy(ref.at[0, pl.ds(2 * s, 2)], mats.at[i], load_sem.at[1 + i])
@@ -73,6 +84,8 @@
         for q in (below, above):
             pl.semaphore_signal(barrier, inc=1, device_id=(q, src), device_id_type=MESH)
 
+    for copy in small_copies:
+        copy.wait()
     side_rows = sbuf.shape[1]
     row_id = lax.broadcasted_iota(jnp.int32, (side_rows, seam), 0)
     for q in range(2):
@@ -101,14 +114,12 @@
     def owner(pair, lev):
         return (2 * pair + lax.rem(lev, 2), lev // 2)
 
+    targets = ((1 - p, (2 * z + 1 - p, s), slot_own), (0, (2 * zn, s), slot_far), (1, (2 * zn + 1, s), slot_far))
+    for i, (q, device, slot) in enumerate(targets):
+        send(sbuf.at[q], side.at[slot], s_send.at[i], s_recv.at[slot], device)
     for d in range(levels):
         lev = lax.rem(own_level + d, levels)
         send(abuf.at[lev], gath.at[slot_far, s], a_send.at[0, d], a_recv.at[slot_far, s], owner(zn, lev))
-        if d > 0:
-            send(abuf.at[lev], gath.at[slot_own, s], a_send.at[1, d], a_recv.at[slot_own, s], owner(z, lev))
-    targets = ((1 - p, (2 * z + 1 - p, s), slot_own), (0, (2 * zn, s), slot_far), (1, (2 * zn + 1, s), slot_far))
-    for i, (q, device, slot) in enumerate(targets):
-        send(sbuf.at[q], side.at[slot], s_send.at[i], s_recv.at[slot], device)
 
     gath[slot_own, s] = abuf[own_level]
     side[slot_own] = sbuf[p]
@@ -128,18 +139,21 @@
                     (row_s >= b * block) & (row_s < (b + 1) * block)
                     & (col_s >= e * block) & (col_s < (e + 1) * block)
                 )
-                present = jnp.where(inside, pattern[0, 2 * s + q, b, e], present)
+                present = jnp.where(inside, pattern[0, b, e, 2 * s + q], present)
         jac_used.append(jnp.where(present == 1, mats[2, q].astype(F32), 0.0).astype(BF16))
-    both = [split(dot(mats[0, q], mats[1, q])) for q in range(2)]
-    g = [dot(both[q][0], jac_used[q]) + dot(both[q][1], jac_used[q]) for q in range(2)]
-    gh = [g[q].astype(BF16) for q in range(2)]
-    acc = [weights[2] * g[q] + weights[3] * dot(gh[q], gh[q]) for q in range(2)]
-    acc = [weights[1] * g[q] + dot(gh[q], acc[q].astype(BF16)) for q in range(2)]
-    acc = [weights[0] * g[q] + dot(gh[q], acc[q].astype(BF16)) for q in range(2)]
+    both = [jnp.concatenate(split(dot(mats[0, q], mats[1, q])), axis=1) for q in range(2)]
+    g = [dot(both[q], twice(jac_used[q])) for q in range(2)]
+    both = [jnp.concatenate(split(g[q]), axis=1) for q in range(2)]
+    acc = [weights[2] * g[q] + weights[3] * dot(both[q], twice(g[q].astype(BF16))) for q in range(2)]
+    acc = [weights[1] * g[q] + dot(both[q], twice(acc[q].astype(BF16))) for q in range(2)]
+    acc = [weights[0] * g[q] + dot(both[q], twice(acc[q].astype(BF16))) for q in range(2)]
     for q in range(2):
         ebuf[q] = jnp.transpose(acc[q]).astype(BF16)
     for i, (q, device, slot) in enumerate(targets):
         send(ebuf.at[q], emat.at[slot], e_send.at[i], e_recv.at[slot], device)
+    for d in range(1, levels):
+        lev = lax.rem(own_level + d, levels)
+        send(abuf.at[lev], gath.at[slot_own, s], a_send.at[1, d], a_recv.at[slot_own, s], owner(z, lev))
     emat[slot_own] = ebuf[p]
 
     def arrived(dst, sem):
@@ -171,16 +185,18 @@
 
     lane = lax.broadcasted_iota(jnp.int32, (1, seam), 1).astype(F32)
 
-    for slot in (slot_other, 0, 3):
-        arrived(emat.at[slot], e_recv.at[slot])
-    for d in range(1, specs):
-        src = lax.rem(s + d, specs)
-        arrived(gath.at[slot_own, src], a_recv.at[slot_own, src])
-    for src in range(specs):
-        for slot in (slot_other, 0, 3):
-            arrived(gath.at[slot, src], a_recv.at[slot, src])
-
     for k in (1, 2, 0, 3):
+        if k == 1:
+            arrived(emat.at[slot_other], e_recv.at[slot_other])
+            for d in range(1, specs):
+                src = lax.rem(s + d, specs)
+                arrived(gath.at[slot_own, src], a_recv.at[slot_own, src])
+            for src in range(specs):
+                arrived(gath.at[slot_other, src], a_recv.at[slot_other, src])
+        elif k != 2:
+            arrived(emat.at[k], e_recv.at[k])
+            for src in range(specs):
+                arrived(gath.at[k, src], a_recv.at[k, src])
         field = [[gath[k, src, r] for src in range(specs)] for r in range(rows)]
         field = [jnp.concatenate(parts, axis=0) for parts in field]
         if k != 1:
@@ -197,10 +213,9 @@
     total = 4 * rows
     group = 16
     shape = (group, seam)
-    per_dev = species_dev // group
-
-    def advect(i, carry):
-        at = pl.multiple_of(i * group, group)
+
+    def advect(who, within):
+        at = pl.multiple_of(who * species_dev + within, group)
         a = [state[r, pl.ds(at, group), :] for r in range(total)]
         for step in range(1, NSUB + 1):
             new = list(a)
@@ -209,29 +224,27 @@
                 falling = jnp.minimum(faces[r - 1], 0.0)
                 new[r] = a[r] + rising * (a[r + 1] - a[r]) + falling * (a[r] - a[r - 1])
             a = new
-        who = i // per_dev
-        within = pl.multiple_of((i - who * per_dev) * group, group)
-        for r in range(rows):
-            ret[0, who, r, pl.ds(within, group), :] = a[rows + r].astype(BF16)
+        for r in range(rows):
+            ret[0, who, r, within : within + group, :] = a[rows + r].astype(BF16)
         upper = jnp.concatenate([a[2 * rows + r] for r in range(rows)], axis=0).astype(BF16)
         upper = dot(upper, perms[2]).astype(BF16)
         for r in range(rows):
-            ret[1, who, r, pl.ds(within, group), :] = upper[r * group : (r + 1) * group]
-        return carry
-
-    lax.fori_loop(0, species // group, advect, 0)
-
+            ret[1, who, r, within : within + group, :] = upper[r * group : (r + 1) * group]
+
+    for i in range(specs):
+        who = lax.rem(s + 1 + i, specs)
+        for within in range(0, species_dev, group):
+            advect(who, within)
+        for j in range(2):
+            q = lax.rem(p + 1 + j, 2)
+            if i < specs - 1 or j == 0:
+                send(ret.at[q, who], out.at[own_level], r_send.at[2 * i + j], r_recv.at[own_level], (2 * z + q, who))
+    own_copy = pltpu.make_async_copy(ret.at[p, s], out.at[own_level], own_sem)
+    own_copy.start()
     for d in range(1, levels):
         lev = lax.rem(own_level + d, levels)
-        q = lax.rem(lev, 2)
-        send(ret.at[q, lev // 2], rbuf.at[own_level], r_send.at[d], r_recv.at[own_level], owner(z, lev))
-    rbuf[own_level] = ret[p, s]
-    for d in range(1, levels):
-        lev = lax.rem(own_level + d, levels)
-        arrived(rbuf.at[lev], r_recv.at[lev])
-    for lev in range(levels):
-        for r in range(rows):
-            out[pl.ds(lev * rows + r, species_dev, stride), :] = rbuf[lev, r].astype(F32)
+        arrived(out.at[lev], r_recv.at[lev])
+    own_copy.wait()
     for copy in sends:
         copy.wait_send()
 
@@ -244,14 +257,16 @@
     dma = pltpu.SemaphoreType.DMA
     out = pl.pallas_call(
         functools.partial(kernel, tiles, specs, levels, rows, species_dev, pattern.shape[2]),
-        out_shape=jax.ShapeDtypeStruct((species_dev * levels * rows, seam), F32),
-        in_specs=[pl.BlockSpec(memory_space=pl.ANY)] * 4
-        + [pl.BlockSpec(memory_space=pltpu.VMEM)]
-        + [pl.BlockSpec(memory_space=pltpu.SMEM)] * 3,
-        out_specs=pl.BlockSpec(memory_space=pltpu.VMEM),
+        out_shape=jax.ShapeDtypeStruct((levels, rows, species_dev, seam), BF16),
+        in_specs=[pl.BlockSpec(memory_space=pl.ANY)] * 8,
+        out_specs=pl.BlockSpec(memory_space=pl.ANY),
         scratch_shapes=[
             pltpu.VMEM((species_dev * levels * rows, seam), F32),
             pltpu.VMEM((3, 2, species, species), BF16),
+            pltpu.VMEM(courant.shape, F32),
+            pltpu.SMEM((1,) + pattern.shape[2:] + (levels,), jnp.int32),
+            pltpu.SMEM(counts.shape, jnp.int32),
+            pltpu.SMEM(seam_codes.shape, jnp.int32),
             pltpu.VMEM((levels, rows, species_dev, seam), BF16),
             pltpu.VMEM((4, specs, rows, species_dev, seam), BF16),
             pltpu.VMEM((2, species, species), BF16),
@@ -260,8 +275,8 @@
             pltpu.VMEM((4, side_rows, seam), F32),
             pltpu.VMEM((4 * rows, species, seam), F32),
             pltpu.VMEM((2, specs, rows, species_dev, seam), BF16),
-            pltpu.VMEM((levels, rows, species_dev, seam), BF16),
-            dma((4,)),
+            dma((8,)),
+            dma(()),
             dma((2, levels)),
             dma((4, specs)),
             dma((3,)),
@@ -272,13 +287,13 @@
             dma((levels,)),
         ],
         compiler_params=pltpu.CompilerParams(
-            collective_id=0, has_side_effects=True, vmem_limit_bytes=32 * 1024 * 1024
+            collective_id=0, has_side_effects=True, vmem_limit_bytes=60 * 1024 * 1024
         ),
     )(
         adjoint.reshape(species_dev * levels * rows, seam),
-        section_first, section_second, jacobian, courant, pattern, counts, seam_codes,
+        section_first, section_second, jacobian, courant, jnp.transpose(pattern, (0, 2, 3, 1)), counts, seam_codes,
     )
-    return out.reshape(species_dev, levels, rows, seam)
+    return jnp.transpose(out, (2, 0, 1, 3)).astype(F32)
 
 
 def solution(mesh):

time: 30.5 us -> 24.7 us (0.81)
  local copies, waits for them, and re-layouts: 6.2 us -> 1.14 us
  Pallas kernels: 24 us -> 22.4 us
  other arithmetic: 0 us -> 1 us
    unnamed x16 -> x0, local copies, waits for them, and re-layouts: 6.2 us -> none
    pallas_call x1, Pallas kernels: 24 us -> 22.4 us  [shards(): pl.pallas_call(functools.partial(kernel, tiles, specs, levels, rows, spec...]
    convert_element_type x0 -> x1, local copies, waits for them, and re-layouts: none -> 1.14 us  [shards(): return jnp.transpose(out, (2, 0, 1, 3)).astype(F32)]
    convert_element_type x0 -> x1, other arithmetic: none -> 1 us  [shards(): return jnp.transpose(out, (2, 0, 1, 3)).astype(F32)]
where the time goes in v2:
time: 24.7 us; the launch traced here: 24.5 us
  Pallas kernels  22.4 us (91%)
  local copies, waits for them, and re-layouts  1.14 us (5%)
  other arithmetic  1 us (4%)
    pallas_call x1, Pallas kernels, shards(): pl.pallas_call(functools.partial(kernel, tiles, specs, levels, rows, spec...  22.4 us
    convert_element_type x1, local copies, waits for them, and re-layouts, shards(): return jnp.transpose(out, (2, 0, 1, 3)).astype(F32)  1.14 us
    convert_element_type x1, other arithmetic, shards(): return jnp.transpose(out, (2, 0, 1, 3)).astype(F32)  1 us

profile of v2, /device:TPU:0, one launch (start us, length us, event | category | flops | bytes accessed | tf_op | source)
XLA Modules:
  0.0 24.5 jit_solution(636394503563866793)
XLA Ops:
  0.0 22.4 %shard_map.82 = bf16[8,4,32,128]{3,2,1,0:T(8,128)(2,1)} custom-call(f32[1024,128]{1,0:T(8,128)} %bitcast.4, bf16[1,8,128,128]{3,2,1,0:T(8,128)(2,1)} %first_hbm.1, bf16[1,8,128,128]{3,2,1,0:T(8,128)(2,1)} %second_hbm.1, bf16[1,8,128,128]{3,2,1,0:T(8,128)(2,1)} %jac_hbm.1, f32[8,4,128]{2,1,0:T(4,128)} %cour_hbm.1, s32[1,2,2,8]{3,2,1,0:T(2,128)} %bitcast.5, ...), custom_call_target="tpu_custom_call" | custom-call | tf_op jit(solution)/shard_map/pallas_call | solution.py:258
  22.4 1.0 %convert_bitcast_fusion = f32[32,8,4,128]{3,0,2,1:T(8,128)S(1)} fusion(bf16[8,4,32,128]{3,2,1,0:T(8,128)(2,1)} %shard_map.82), kind=kLoop, calls=%fused_computation | loop fusion | flops 131072 | bytes 786432 | tf_op jit(solution)/shard_map/convert_element_type | solution.py:296
  23.4 1.1 %copy.9 = f32[32,8,4,128]{3,2,1,0:T(4,128)} copy(f32[32,8,4,128]{3,0,2,1:T(8,128)S(1)} %convert_bitcast_fusion) | data formatting | bytes 1048576 | tf_op jit(solution)/shard_map/convert_element_type | solution.py:296

commit v3 on v2

--- a/solution.py
+++ b/solution.py
@@ -247,6 +247,12 @@
     own_copy.wait()
     for copy in sends:
         copy.wait_send()
+
+
+def unpack(levels, rows, part, packed, out):
+    for lev in range(levels):
+        for r in range(rows):
+            out[pl.ds(lev * rows + r, part, levels * rows), :] = packed[lev, r].astype(F32)
 
 
 def shards(tiles, specs, adjoint, section_first, section_second, jacobian, pattern, counts, courant, seam_codes):
@@ -293,7 +299,18 @@
         adjoint.reshape(species_dev * levels * rows, seam),
         section_first, section_second, jacobian, courant, jnp.transpose(pattern, (0, 2, 3, 1)), counts, seam_codes,
     )
-    return jnp.transpose(out, (2, 0, 1, 3)).astype(F32)
+    halves = 2
+    part = species_dev // halves
+    size = levels * rows
+    final = pl.pallas_call(
+        functools.partial(unpack, levels, rows, part),
+        grid=(halves,),
+        out_shape=jax.ShapeDtypeStruct((species_dev * size, seam), F32),
+        in_specs=[pl.BlockSpec((levels, rows, part, seam), lambda i: (0, 0, i, 0))],
+        out_specs=pl.BlockSpec((part * size, seam), lambda i: (i, 0)),
+        cost_estimate=pl.CostEstimate(flops=0, bytes_accessed=6 * species_dev * size * seam, transcendentals=0),
+    )(out)
+    return final.reshape(species_dev, levels, rows, seam)
 
 
 def solution(mesh):

time: 24.7 us -> 24.6 us (level)
  Pallas kernels: 22.4 us -> 24.4 us
  local copies, waits for them, and re-layouts: 1.14 us -> 0 us
  other arithmetic: 1 us -> 0 us
    pallas_call x0 -> x1, Pallas kernels: none -> 2.05 us  [shards(): pl.pallas_call(functools.partial(unpack, levels, rows, part), grid=(halve...]
    convert_element_type x1 -> x0, local copies, waits for them, and re-layouts: 1.14 us -> none  [shards(): return jnp.transpose(out, (2, 0, 1, 3)).astype(F32)]
    convert_element_type x1 -> x0, other arithmetic: 1 us -> none  [shards(): return jnp.transpose(out, (2, 0, 1, 3)).astype(F32)]
where the time goes in v3:
time: 24.6 us; the launch traced here: 24.4 us
  Pallas kernels  24.4 us (99%)
    pallas_call x1, Pallas kernels, shards(): pl.pallas_call(functools.partial(kernel, tiles, specs, levels, rows, spec...  22.4 us
    pallas_call x1, Pallas kernels, shards(): pl.pallas_call(functools.partial(unpack, levels, rows, part), grid=(halve...  2.05 us

profile of v3, /device:TPU:0, one launch (start us, length us, event | category | flops | bytes accessed | tf_op | source)
XLA Modules:
  0.0 24.4 jit_solution(18189081708801118273)
XLA Ops:
  0.0 22.4 %shard_map.82.packed = bf16[8,4,32,128]{3,2,1,0:T(8,128)(2,1)} custom-call(f32[1024,128]{1,0:T(8,128)} %bitcast.3, bf16[1,8,128,128]{3,2,1,0:T(8,128)(2,1)} %first_hbm.1, bf16[1,8,128,128]{3,2,1,0:T(8,128)(2,1)} %second_hbm.1, bf16[1,8,128,128]{3,2,1,0:T(8,128)(2,1)} %jac_hbm.1, f32[8,4,128]{2,1,0:T(4,128)} %cour_hbm.1, s32[1,2,2,8]{3,2,1,0:T(2,128)} %bitcast.4, ...), custom_call_target="tpu_custom_call" | custom-call | tf_op jit(solution)/shard_map/pallas_call | solution.py:264
  22.4 2.1 %shard_map.83 = f32[1024,128]{1,0:T(8,128)} custom-call(bf16[8,4,32,128]{3,2,1,0:T(8,128)(2,1)} %shard_map.82.packed), custom_call_target="tpu_custom_call" | custom-call | bytes 786432 | tf_op jit(solution)/shard_map/pallas_call | solution.py:305

commit v4 on v2

--- a/solution.py
+++ b/solution.py
@@ -59,18 +59,24 @@
     slot_far = 3 * (1 - p)
     own_level = 2 * s + p
 
-    adj_copy = pltpu.make_async_copy(adj_hbm, adj, load_sem.at[0])
-    adj_copy.start()
+    halves = 2
+    part = species_dev // halves
+    adj_copies = []
+    for h in range(halves):
+        span = pl.ds(h * part * stride, part * stride)
+        copy = pltpu.make_async_copy(adj_hbm.at[span], adj.at[span], load_sem.at[h])
+        copy.start()
+        adj_copies.append(copy)
     small_copies = []
     for i, (ref, to) in enumerate(
         ((cour_hbm, cour), (counts_hbm, counts), (codes_hbm, codes), (pattern_hbm, pattern))
     ):
-        copy = pltpu.make_async_copy(ref, to, load_sem.at[4 + i])
+        copy = pltpu.make_async_copy(ref, to, load_sem.at[2 + i])
         copy.start()
         small_copies.append(copy)
     mat_copies = []
     for i, ref in enumerate((first_hbm, second_hbm, jac_hbm)):
-        copy = pltpu.make_async_copy(ref.at[0, pl.ds(2 * s, 2)], mats.at[i], load_sem.at[1 + i])
+        copy = pltpu.make_async_copy(ref.at[0, pl.ds(2 * s, 2)], mats.at[i], load_sem.at[6 + i])
         copy.start()
         mat_copies.append(copy)
 
@@ -94,10 +100,12 @@
         packed = jnp.where(row_id == rows + 2, counts[0, 2 * s + q].astype(F32), packed)
         sbuf[q] = packed
         sbuf[q, 0:rows, :] = cour[2 * s + q]
-    adj_copy.wait()
-    for lev in range(levels):
-        for r in range(rows):
-            abuf[lev, r] = adj[pl.ds(lev * rows + r, species_dev, stride), :].astype(BF16)
+    for h in range(halves):
+        adj_copies[h].wait()
+        for lev in range(levels):
+            for r in range(rows):
+                start = h * part * stride + lev * rows + r
+                abuf[lev, r, h * part : (h + 1) * part, :] = adj[pl.ds(start, part, stride), :].astype(BF16)
 
     pl.semaphore_wait(barrier, 2 * levels - 1)
 
@@ -121,6 +129,9 @@
         lev = lax.rem(own_level + d, levels)
         send(abuf.at[lev], gath.at[slot_far, s], a_send.at[0, d], a_recv.at[slot_far, s], owner(zn, lev))
 
+    for d in range(1, levels):
+        lev = lax.rem(own_level + d, levels)
+        send(abuf.at[lev], gath.at[slot_own, s], a_send.at[1, d], a_recv.at[slot_own, s], owner(z, lev))
     gath[slot_own, s] = abuf[own_level]
     side[slot_own] = sbuf[p]
 
@@ -151,9 +162,6 @@
         ebuf[q] = jnp.transpose(acc[q]).astype(BF16)
     for i, (q, device, slot) in enumerate(targets):
         send(ebuf.at[q], emat.at[slot], e_send.at[i], e_recv.at[slot], device)
-    for d in range(1, levels):
-        lev = lax.rem(own_level + d, levels)
-        send(abuf.at[lev], gath.at[slot_own, s], a_send.at[1, d], a_recv.at[slot_own, s], owner(z, lev))
     emat[slot_own] = ebuf[p]
 
     def arrived(dst, sem):
@@ -247,6 +255,32 @@
     own_copy.wait()
     for copy in sends:
         copy.wait_send()
+
+
+def unpack(packed_hbm, out_hbm, packed, out, in_sem, out_sem):
+    levels, rows, species_dev, seam = packed.shape
+    halves = 2
+    part = species_dev // halves
+    stride = levels * rows
+    loads = []
+    for h in range(halves):
+        span = pl.ds(h * part, part)
+        copy = pltpu.make_async_copy(packed_hbm.at[:, :, span], packed.at[:, :, span], in_sem.at[h])
+        copy.start()
+        loads.append(copy)
+    stores = []
+    for h in range(halves):
+        loads[h].wait()
+        for lev in range(levels):
+            for r in range(rows):
+                start = h * part * stride + lev * rows + r
+                out[pl.ds(start, part, stride), :] = packed[lev, r, h * part : (h + 1) * part, :].astype(F32)
+        span = pl.ds(h * part * stride, part * stride)
+        copy = pltpu.make_async_copy(out.at[span], out_hbm.at[span], out_sem.at[h])
+        copy.start()
+        stores.append(copy)
+    for copy in stores:
+        copy.wait()
 
 
 def shards(tiles, specs, adjoint, section_first, section_second, jacobian, pattern, counts, courant, seam_codes):
@@ -275,7 +309,7 @@
             pltpu.VMEM((4, side_rows, seam), F32),
             pltpu.VMEM((4 * rows, species, seam), F32),
             pltpu.VMEM((2, specs, rows, species_dev, seam), BF16),
-            dma((8,)),
+            dma((9,)),
             dma(()),
             dma((2, levels)),
             dma((4, specs)),
@@ -293,7 +327,22 @@
         adjoint.reshape(species_dev * levels * rows, seam),
         section_first, section_second, jacobian, courant, jnp.transpose(pattern, (0, 2, 3, 1)), counts, seam_codes,
     )
-    return jnp.transpose(out, (2, 0, 1, 3)).astype(F32)
+    size = species_dev * levels * rows
+    final = pl.pallas_call(
+        unpack,
+        out_shape=jax.ShapeDtypeStruct((size, seam), F32),
+        in_specs=[pl.BlockSpec(memory_space=pl.ANY)],
+        out_specs=pl.BlockSpec(memory_space=pl.ANY),
+        scratch_shapes=[
+            pltpu.VMEM((levels, rows, species_dev, seam), BF16),
+            pltpu.VMEM((size, seam), F32),
+            dma((2,)),
+            dma((2,)),
+        ],
+        compiler_params=pltpu.CompilerParams(vmem_limit_bytes=60 * 1024 * 1024),
+        cost_estimate=pl.CostEstimate(flops=0, bytes_accessed=6 * size * seam, transcendentals=0),
+    )(out)
+    return final.reshape(species_dev, levels, rows, seam)
 
 
 def solution(mesh):

time: 24.7 us -> 24.1 us (0.976)
  Pallas kernels: 22.4 us -> 23.9 us
  local copies, waits for them, and re-layouts: 1.14 us -> 0 us
  other arithmetic: 1 us -> 0 us
    pallas_call x0 -> x1, Pallas kernels: none -> 2.08 us  [shards(): pl.pallas_call(unpack, out_shape=jax.ShapeDtypeStruct((size, seam), F32),...]
    convert_element_type x1 -> x0, local copies, waits for them, and re-layouts: 1.14 us -> none  [shards(): return jnp.transpose(out, (2, 0, 1, 3)).astype(F32)]
    convert_element_type x1 -> x0, other arithmetic: 1 us -> none  [shards(): return jnp.transpose(out, (2, 0, 1, 3)).astype(F32)]
    pallas_call x1, Pallas kernels: 22.4 us -> 21.8 us  [shards(): pl.pallas_call(functools.partial(kernel, tiles, specs, levels, rows, spec...]
where the time goes in v4:
time: 24.1 us; the launch traced here: 23.9 us
  Pallas kernels  23.9 us (99%)
    pallas_call x1, Pallas kernels, shards(): pl.pallas_call(functools.partial(kernel, tiles, specs, levels, rows, spec...  21.8 us
    pallas_call x1, Pallas kernels, shards(): pl.pallas_call(unpack, out_shape=jax.ShapeDtypeStruct((size, seam), F32),...  2.08 us

profile of v4, /device:TPU:0, one launch (start us, length us, event | category | flops | bytes accessed | tf_op | source)
XLA Modules:
  0.0 23.9 jit_solution(679789548408073985)
XLA Ops:
  0.0 21.8 %shard_map.82.packed_hbm = bf16[8,4,32,128]{3,2,1,0:T(8,128)(2,1)} custom-call(f32[1024,128]{1,0:T(8,128)} %bitcast.3, bf16[1,8,128,128]{3,2,1,0:T(8,128)(2,1)} %first_hbm.1, bf16[1,8,128,128]{3,2,1,0:T(8,128)(2,1)} %second_hbm.1, bf16[1,8,128,128]{3,2,1,0:T(8,128)(2,1)} %jac_hbm.1, f32[8,4,128]{2,1,0:T(4,128)} %cour_hbm.1, s32[1,2,2,8]{3,2,1,0:T(2,128)} %bitcast.4, ...), custom_call_target="tpu_custom_call" | custom-call | tf_op jit(solution)/shard_map/pallas_call | solution.py:292
  21.8 2.1 %shard_map.83 = f32[1024,128]{1,0:T(8,128)} custom-call(bf16[8,4,32,128]{3,2,1,0:T(8,128)(2,1)} %shard_map.82.packed_hbm), custom_call_target="tpu_custom_call" | custom-call | bytes 786432 | tf_op jit(solution)/shard_map/pallas_call | solution.py:331

commit v5 on v4

--- a/solution.py
+++ b/solution.py
@@ -15,6 +15,11 @@
 MESH = pl.DeviceIdType.MESH
 F32 = jnp.float32
 BF16 = jnp.bfloat16
+
+
+def padded_pitch(count):
+    tiles = (count + 7) // 8
+    return 8 * (tiles + 1 - tiles % 2)
 
 
 def power_weights():
@@ -48,6 +53,7 @@
     species = specs * species_dev
     cells = rows * seam
     stride = levels * rows
+    pitch = padded_pitch(stride)
     pairs = tiles // 2
     t = lax.axis_index("tile")
     s = lax.axis_index("spec")
@@ -63,8 +69,10 @@
     part = species_dev // halves
     adj_copies = []
     for h in range(halves):
-        span = pl.ds(h * part * stride, part * stride)
-        copy = pltpu.make_async_copy(adj_hbm.at[span], adj.at[span], load_sem.at[h])
+        span = pl.ds(h * part, part)
+        copy = pltpu.make_async_copy(
+            adj_hbm.at[span], adj.reshape(species_dev, pitch, seam).at[span, pl.ds(0, stride)], load_sem.at[h]
+        )
         copy.start()
         adj_copies.append(copy)
     small_copies = []
@@ -104,8 +112,8 @@
         adj_copies[h].wait()
         for lev in range(levels):
             for r in range(rows):
-                start = h * part * stride + lev * rows + r
-                abuf[lev, r, h * part : (h + 1) * part, :] = adj[pl.ds(start, part, stride), :].astype(BF16)
+                start = h * part * pitch + lev * rows + r
+                abuf[lev, r, h * part : (h + 1) * part, :] = adj[pl.ds(start, part, pitch), :].astype(BF16)
 
     pl.semaphore_wait(barrier, 2 * levels - 1)
 
@@ -262,6 +270,7 @@
     halves = 2
     part = species_dev // halves
     stride = levels * rows
+    pitch = padded_pitch(stride)
     loads = []
     for h in range(halves):
         span = pl.ds(h * part, part)
@@ -273,10 +282,12 @@
         loads[h].wait()
         for lev in range(levels):
             for r in range(rows):
-                start = h * part * stride + lev * rows + r
-                out[pl.ds(start, part, stride), :] = packed[lev, r, h * part : (h + 1) * part, :].astype(F32)
-        span = pl.ds(h * part * stride, part * stride)
-        copy = pltpu.make_async_copy(out.at[span], out_hbm.at[span], out_sem.at[h])
+                start = h * part * pitch + lev * rows + r
+                out[pl.ds(start, part, pitch), :] = packed[lev, r, h * part : (h + 1) * part, :].astype(F32)
+        span = pl.ds(h * part, part)
+        copy = pltpu.make_async_copy(
+            out.reshape(species_dev, pitch, seam).at[span, pl.ds(0, stride)], out_hbm.at[span], out_sem.at[h]
+        )
         copy.start()
         stores.append(copy)
     for copy in stores:
@@ -295,7 +306,7 @@
         in_specs=[pl.BlockSpec(memory_space=pl.ANY)] * 8,
         out_specs=pl.BlockSpec(memory_space=pl.ANY),
         scratch_shapes=[
-            pltpu.VMEM((species_dev * levels * rows, seam), F32),
+            pltpu.VMEM((species_dev * padded_pitch(levels * rows), seam), F32),
             pltpu.VMEM((3, 2, species, species), BF16),
             pltpu.VMEM(courant.shape, F32),
             pltpu.SMEM((1,) + pattern.shape[2:] + (levels,), jnp.int32),
@@ -324,18 +335,18 @@
             collective_id=0, has_side_effects=True, vmem_limit_bytes=60 * 1024 * 1024
         ),
     )(
-        adjoint.reshape(species_dev * levels * rows, seam),
+        adjoint.reshape(species_dev, levels * rows, seam),
         section_first, section_second, jacobian, courant, jnp.transpose(pattern, (0, 2, 3, 1)), counts, seam_codes,
     )
     size = species_dev * levels * rows
     final = pl.pallas_call(
         unpack,
-        out_shape=jax.ShapeDtypeStruct((size, seam), F32),
+        out_shape=jax.ShapeDtypeStruct((species_dev, levels * rows, seam), F32),
         in_specs=[pl.BlockSpec(memory_space=pl.ANY)],
         out_specs=pl.BlockSpec(memory_space=pl.ANY),
         scratch_shapes=[
             pltpu.VMEM((levels, rows, species_dev, seam), BF16),
-            pltpu.VMEM((size, seam), F32),
+            pltpu.VMEM((species_dev * padded_pitch(levels * rows), seam), F32),
             dma((2,)),
             dma((2,)),
         ],

time: 24.1 us -> 23.8 us (0.988)
  Pallas kernels: 23.9 us -> 23.6 us
    pallas_call x1, Pallas kernels: 2.08 us -> 1.77 us  [shards(): pl.pallas_call(unpack, out_shape=jax.ShapeDtypeStruct((species_dev, level...]
where the time goes in v5:
time: 23.8 us; the launch traced here: 23.6 us
  Pallas kernels  23.6 us (99%)
    pallas_call x1, Pallas kernels, shards(): pl.pallas_call(functools.partial(kernel, tiles, specs, levels, rows, spec...  21.8 us
    pallas_call x1, Pallas kernels, shards(): pl.pallas_call(unpack, out_shape=jax.ShapeDtypeStruct((species_dev, level...  1.77 us

profile of v5, /device:TPU:0, one launch (start us, length us, event | category | flops | bytes accessed | tf_op | source)
XLA Modules:
  0.0 23.6 jit_solution(3786339166330529955)
XLA Ops:
  0.0 21.8 %shard_map.82.packed_hbm = bf16[8,4,32,128]{3,2,1,0:T(8,128)(2,1)} custom-call(f32[32,32,128]{2,1,0:T(8,128)} %bitcast.3, bf16[1,8,128,128]{3,2,1,0:T(8,128)(2,1)} %first_hbm.1, bf16[1,8,128,128]{3,2,1,0:T(8,128)(2,1)} %second_hbm.1, bf16[1,8,128,128]{3,2,1,0:T(8,128)(2,1)} %jac_hbm.1, f32[8,4,128]{2,1,0:T(4,128)} %cour_hbm.1, s32[1,2,2,8]{3,2,1,0:T(2,128)} %bitcast.4, ...), custom_call_target="tpu_custom_call" | custom-call | tf_op jit(solution)/shard_map/pallas_call | solution.py:303
  21.8 1.8 %shard_map.83 = f32[32,32,128]{2,1,0:T(8,128)} custom-call(bf16[8,4,32,128]{3,2,1,0:T(8,128)(2,1)} %shard_map.82.packed_hbm), custom_call_target="tpu_custom_call" | custom-call | bytes 786432 | tf_op jit(solution)/shard_map/pallas_call | solution.py:342

commit v6 on v5

--- a/solution.py
+++ b/solution.py
@@ -272,15 +272,15 @@
     stride = levels * rows
     pitch = padded_pitch(stride)
     loads = []
-    for h in range(halves):
-        span = pl.ds(h * part, part)
-        copy = pltpu.make_async_copy(packed_hbm.at[:, :, span], packed.at[:, :, span], in_sem.at[h])
+    for lev in range(levels):
+        copy = pltpu.make_async_copy(packed_hbm.at[lev], packed.at[lev], in_sem.at[lev])
         copy.start()
         loads.append(copy)
     stores = []
     for h in range(halves):
-        loads[h].wait()
         for lev in range(levels):
+            if h == 0:
+                loads[lev].wait()
             for r in range(rows):
                 start = h * part * pitch + lev * rows + r
                 out[pl.ds(start, part, pitch), :] = packed[lev, r, h * part : (h + 1) * part, :].astype(F32)
@@ -347,7 +347,7 @@
         scratch_shapes=[
             pltpu.VMEM((levels, rows, species_dev, seam), BF16),
             pltpu.VMEM((species_dev * padded_pitch(levels * rows), seam), F32),
-            dma((2,)),
+            dma((levels,)),
             dma((2,)),
         ],
         compiler_params=pltpu.CompilerParams(vmem_limit_bytes=60 * 1024 * 1024),

time: 23.8 us -> 23.8 us (level)
  no operation moved by 1% of the time
where the time goes in v6:
time: 23.8 us; the launch traced here: 23.6 us
  Pallas kernels  23.6 us (99%)
    pallas_call x1, Pallas kernels, shards(): pl.pallas_call(functools.partial(kernel, tiles, specs, levels, rows, spec...  21.8 us
    pallas_call x1, Pallas kernels, shards(): pl.pallas_call(unpack, out_shape=jax.ShapeDtypeStruct((species_dev, level...  1.75 us

profile of v6, /device:TPU:0, one launch (start us, length us, event | category | flops | bytes accessed | tf_op | source)
XLA Modules:
  0.0 23.6 jit_solution(16560937774065911561)
XLA Ops:
  0.0 21.8 %shard_map.82.packed_hbm = bf16[8,4,32,128]{3,2,1,0:T(8,128)(2,1)} custom-call(f32[32,32,128]{2,1,0:T(8,128)} %bitcast.3, bf16[1,8,128,128]{3,2,1,0:T(8,128)(2,1)} %first_hbm.1, bf16[1,8,128,128]{3,2,1,0:T(8,128)(2,1)} %second_hbm.1, bf16[1,8,128,128]{3,2,1,0:T(8,128)(2,1)} %jac_hbm.1, f32[8,4,128]{2,1,0:T(4,128)} %cour_hbm.1, s32[1,2,2,8]{3,2,1,0:T(2,128)} %bitcast.4, ...), custom_call_target="tpu_custom_call" | custom-call | tf_op jit(solution)/shard_map/pallas_call | solution.py:303
  21.8 1.8 %shard_map.83 = f32[32,32,128]{2,1,0:T(8,128)} custom-call(bf16[8,4,32,128]{3,2,1,0:T(8,128)(2,1)} %shard_map.82.packed_hbm), custom_call_target="tpu_custom_call" | custom-call | bytes 786432 | tf_op jit(solution)/shard_map/pallas_call | solution.py:342
